TPU v7x, 256 devices: a whole 4x4x8 slice. The times are simulated.
256 devices in a mesh: year: 8 (over z), row: 8 (over x, core), col: 4 (over y).
Axes of the slice: x: 4, y: 4, z: 8, core: 2. Of those that a mesh axis runs over, the one named last changes fastest.
Arguments:
- observed: float32 [8, 46, 512, 512], P('year', None, 'row', 'col'), may hold values from 0 to 0.8
- quality: int32 [8, 46, 512, 512], P('year', None, 'row', 'col'), may hold values from 0 to 3, as said below
- land_mask: int32 [512, 512], P('row', 'col'), may hold values 0 or 1
- params: float32 [8, 7, 512, 512], P('year', None, 'row', 'col'), may hold values from -0.3 to 3.4
- spatial_weight: float32 [7], replicated, may hold values from 0.2 to 2
- temporal_weight: float32 [7], replicated, may hold values from 0.2 to 2
Outputs:
- new_params: float32 [8, 7, 512, 512], P('year', None, 'row', 'col')
- residual: float32 [8, 7, 512, 512], P('year', None, 'row', 'col')
Inputs may be any that keep to these rules, and one draw needn't show every extreme that they name: `quality`: 0 good, 1 marginal, 2 snow, 3 cloud.
All inputs are finite; a program needn't handle non-finite values. No bound on the sum of `land_mask` on one device may be relied on, other than what follows from the above.
Results may differ from a plain program's by a relative error of at most 0.0003.
Values sent between devices are 32-bit elements; how exact they have to be, the bound alone decides.
No kernel may reach another device: no remote copies, remote signals or barrier semaphores. Data moves between devices by JAX's collectives and lax.ppermute only.
A program may use at most 64 MiB of HBM per device.

v0:
```python
import jax
import jax.numpy as jnp
from jax import lax
from jax.sharding import PartitionSpec as P

ITERS = 4


damping = 0.1


def with_halo(cells, sides, width):
    for axis, dim in sides:
        count = lax.axis_size(axis)
        ends = count - 1
        head = lax.slice_in_dim(cells, 0, width, axis=dim)
        tail = lax.slice_in_dim(cells, cells.shape[dim] - width, cells.shape[dim], axis=dim)
        cells = jnp.concatenate(
            [
                lax.ppermute(tail, axis, [(i, (i + 1) % count) for i in range(ends)]),
                cells,
                lax.ppermute(head, axis, [((i + 1) % count, i) for i in range(ends)]),
            ],
            axis=dim,
        )
    return cells


def upper_pairs(count):
    return [
        (left_index, right_index)
        for left_index in range(count)
        for right_index in range(left_index, count)
    ]


def curve_terms(observed, quality, land_mask, params):
    num_dates = observed.shape[1]
    count = params.shape[1]
    weight = jnp.where(quality == 0, 1.0, 0.0) + jnp.where(quality == 1, 0.5, 0.0)
    weight = weight * land_mask.astype(jnp.float32)[None, None] / num_dates
    date_times = (jnp.arange(num_dates, dtype=jnp.float32) / num_dates).reshape(1, num_dates, 1, 1)
    level_base, peak_value, green_slope, rise_mid, rise_log, fall_mid, fall_log = [
        params[:, index][:, None] for index in range(count)
    ]
    rise_rate = jnp.exp(rise_log)
    fall_rate = jnp.exp(fall_log)
    rise_curve = jax.nn.sigmoid(rise_rate * (date_times - rise_mid))
    fall_curve = jax.nn.sigmoid(fall_rate * (date_times - fall_mid))
    season = rise_curve - fall_curve
    amplitude = peak_value - green_slope * date_times
    misfit = level_base + amplitude * season - observed
    rise_slope = rise_curve * (1.0 - rise_curve)
    fall_slope = fall_curve * (1.0 - fall_curve)
    jacobian = [
        jnp.ones_like(misfit),
        season,
        -date_times * season,
        -amplitude * rise_rate * rise_slope,
        amplitude * rise_slope * (date_times - rise_mid) * rise_rate,
        amplitude * fall_rate * fall_slope,
        -amplitude * fall_slope * (date_times - fall_mid) * fall_rate,
    ]
    weighted = [weight * column for column in jacobian]
    hessian = jnp.stack(
        [
            jnp.sum(weighted[left_index] * jacobian[right_index], axis=1)
            for left_index, right_index in upper_pairs(count)
        ]
    )
    gradient = jnp.stack(
        [jnp.sum(weighted[index] * misfit, axis=1) for index in range(count)], axis=1
    )
    return (hessian, gradient)


def blocks_from(hessian, count):
    blocks = [[None] * count for index in range(count)]
    for position, (left_index, right_index) in enumerate(upper_pairs(count)):
        blocks[left_index][right_index] = hessian[position]
        blocks[right_index][left_index] = hessian[position]
    return blocks


def block_apply(blocks, field):
    count = len(blocks)
    outputs = []
    for left_index in range(count):
        total = blocks[left_index][0] * field[:, 0]
        for right_index in range(1, count):
            total = total + blocks[left_index][right_index] * field[:, right_index]
        outputs.append(total)
    return jnp.stack(outputs, axis=1)


def invert(blocks):
    count = len(blocks)
    left_rows = [list(row) for row in blocks]
    right_rows = [
        [
            jnp.full_like(blocks[0][0], 1.0 if left_index == right_index else 0.0)
            for right_index in range(count)
        ]
        for left_index in range(count)
    ]
    for pivot in range(count):
        scale = 1.0 / left_rows[pivot][pivot]
        left_rows[pivot] = [entry * scale for entry in left_rows[pivot]]
        right_rows[pivot] = [entry * scale for entry in right_rows[pivot]]
        for other in range(count):
            if other != pivot:
                factor = left_rows[other][pivot]
                left_rows[other] = [
                    entry - factor * base_entry
                    for entry, base_entry in zip(left_rows[other], left_rows[pivot])
                ]
                right_rows[other] = [
                    entry - factor * base_entry
                    for entry, base_entry in zip(right_rows[other], right_rows[pivot])
                ]
    return right_rows


def prior_apply(field, spatial_weight, temporal_weight):
    num_years = field.shape[0]
    num_rows = field.shape[2]
    num_cols = field.shape[3]
    padded = with_halo(field, (("year", 0), ("row", 2), ("col", 3)), 1)
    year_pad = padded[:, :, 1:-1, 1:-1]
    plane_pad = padded[1:-1]
    year_pos = (
        lax.broadcasted_iota(jnp.int32, (num_years, 1, 1, 1), 0)
        + lax.axis_index("year") * num_years
    )
    row_pos = (
        lax.broadcasted_iota(jnp.int32, (1, 1, num_rows, 1), 2) + lax.axis_index("row") * num_rows
    )
    col_pos = (
        lax.broadcasted_iota(jnp.int32, (1, 1, 1, num_cols), 3) + lax.axis_index("col") * num_cols
    )
    year_low = jnp.where(year_pos == 0, field, year_pad[:-2])
    year_high = jnp.where(year_pos == num_years * lax.axis_size("year") - 1, field, year_pad[2:])
    row_low = jnp.where(row_pos == 0, field, plane_pad[:, :, :-2, 1:-1])
    row_high = jnp.where(
        row_pos == num_rows * lax.axis_size("row") - 1, field, plane_pad[:, :, 2:, 1:-1]
    )
    col_low = jnp.where(col_pos == 0, field, plane_pad[:, :, 1:-1, :-2])
    col_high = jnp.where(
        col_pos == num_cols * lax.axis_size("col") - 1, field, plane_pad[:, :, 1:-1, 2:]
    )
    plane = 4.0 * field - (row_low + row_high + col_low + col_high)
    yearly = 2.0 * field - (year_low + year_high)
    return (
        spatial_weight[None, :, None, None] * plane + temporal_weight[None, :, None, None] * yearly
    )


def inner_total(left_field, right_field):
    return lax.psum(jnp.sum(left_field * right_field), ("year", "row", "col"))


def per_device(observed, quality, land_mask, params, spatial_weight, temporal_weight):
    count = params.shape[1]
    hessian, data_grad = curve_terms(observed, quality, land_mask, params)
    blocks = blocks_from(hessian, count)
    shifted = [list(row) for row in blocks]
    for index in range(count):
        shifted[index][index] = blocks[index][index] + (
            damping + 4.0 * spatial_weight[index] + 2.0 * temporal_weight[index]
        )
    precond = invert(shifted)
    residual = -(data_grad + prior_apply(params, spatial_weight, temporal_weight))
    step_field = jnp.zeros_like(params)
    search = block_apply(precond, residual)
    direction = search
    inner_now = inner_total(residual, search)
    for sweep in range(ITERS):
        image = (
            block_apply(blocks, direction)
            + damping * direction
            + prior_apply(direction, spatial_weight, temporal_weight)
        )
        step_len = inner_now / lax.psum(jnp.sum(direction * image), ("year", "row", "col"))
        step_field = step_field + step_len * direction
        residual = residual - step_len * image
        if sweep + 1 < ITERS:
            search = block_apply(precond, residual)
            inner_next = inner_total(residual, search)
            direction = search + inner_next / inner_now * direction
            inner_now = inner_next
    return (params + step_field, residual)


def solution(mesh):
    return jax.shard_map(
        per_device,
        mesh=mesh,
        in_specs=(
            P("year", None, "row", "col"),
            P("year", None, "row", "col"),
            P("row", "col"),
            P("year", None, "row", "col"),
            P(),
            P(),
        ),
        out_specs=(P("year", None, "row", "col"), P("year", None, "row", "col")),
        check_vma=False,
    )
```

profile of v0, /device:TPU:1, one launch (start us, length us, event | category | flops | bytes accessed | tf_op | source)
XLA Modules:
  0.0 745.8 jit_solution(3801507405217815342)
XLA Ops:
  1.9 5.0 collective-permute-start
  7.9 1.5 fusion.376
  13.7 1.5 fusion.375
  20.3 7.8 %multiply_reduce_fusion.21 = (f32[64,128]{1,0:T(8,128)S(1)}, f32[64,128]{1,0:T(8,128)S(1)}, f32[64,128]{1,0:T(8,128)S(1)}, f32[64,128]{1,0:T(8,128)S(1)}, f32[64...) fusion(f32[64,128]{1,0:T(8,128)S(1)} %get-tuple-element.221, ...), kind=kLoop, calls=%fused_computation.37 | loop fusion | flops 40411136 | bytes 4424048 | tf_op jit(solution)/shard_map/reduce_sum | solution.py:72
  37.6 4.7 collective-permute-start.3
  42.3 1.9 collective-permute-start.2
  46.6 1.5 copy.78
  48.4 1.3 collective-permute-start.5
  49.7 4.0 collective-permute-start.4
  56.6 1.6 fusion.67
  58.5 2.7 constant_dynamic-update-slice_fusion.23
  63.4 4.0 collective-permute-start.6
  67.5 2.4 collective-permute-done.7
  70.8 4.4 collective-permute-start.9
  75.2 3.3 collective-permute-start.8
  81.2 3.9 collective-permute-start.10
  87.2 2.8 collective-permute-done.11
  91.1 2.8 multiply_reduce_fusion.34
  94.1 81.9 %all-reduce = (f32[]{:T(128)}, f32[]{:T(128)}) all-reduce(f32[]{:T(128)} %get-tuple-element.40, f32[]{:T(128)} %get-tuple-element.39), channel_id=1, replica_groups=mesh['year'=8,'row'=8,'col'=4] {'year','row','col'}, use_global_device_ids=true, to_apply=%region_36.37 | all-reduce | flops 2 | bytes 16 | tf_op jit(solution)/shard_map/psum | solution.py:159
  181.5 73.8 %psum.58 = f32[]{:T(128)} all-reduce(f32[]{:T(128)} %multiply_reduce_fusion.33), channel_id=1, replica_groups=mesh['year'=8,'row'=8,'col'=4] {'year','row','col'}, use_global_device_ids=true, to_apply=%region_40.41 | all-reduce | flops 1 | bytes 8 | tf_op jit(solution)/shard_map/psum | solution.py:159
  258.0 4.0 collective-permute-start.12
  262.2 2.9 collective-permute-done.13
  266.0 3.8 collective-permute-start.15
  269.8 2.0 collective-permute-start.14
  276.4 4.0 collective-permute-start.16
  280.4 1.4 constant_dynamic-update-slice_fusion.31
  283.3 2.9 multiply_reduce_fusion.32
  286.4 76.7 %psum.59 = f32[]{:T(128)} all-reduce(f32[]{:T(128)} %get-tuple-element.47), channel_id=1, replica_groups=mesh['year'=8,'row'=8,'col'=4] {'year','row','col'}, use_global_device_ids=true, to_apply=%region_42.43 | all-reduce | flops 1 | bytes 8 | tf_op jit(solution)/shard_map/psum | solution.py:183
  368.5 75.1 %psum.60 = f32[]{:T(128)} all-reduce(f32[]{:T(128)} %multiply_reduce_fusion.31), channel_id=1, replica_groups=mesh['year'=8,'row'=8,'col'=4] {'year','row','col'}, use_global_device_ids=true, to_apply=%region_44.45 | all-reduce | flops 1 | bytes 8 | tf_op jit(solution)/shard_map/psum | solution.py:159
  446.3 4.0 collective-permute-start.18
  450.4 2.9 collective-permute-done.19
  454.3 3.8 collective-permute-start.21
  458.0 2.5 collective-permute-start.20
  463.1 2.1 copy.108
  467.4 4.6 collective-permute-start.22
  473.6 1.9 copy.111
  475.5 2.1 multiply_reduce_fusion.30
  477.7 77.0 %psum.61 = f32[]{:T(128)} all-reduce(f32[]{:T(128)} %get-tuple-element.45), channel_id=1, replica_groups=mesh['year'=8,'row'=8,'col'=4] {'year','row','col'}, use_global_device_ids=true, to_apply=%region_46.47 | all-reduce | flops 1 | bytes 8 | tf_op jit(solution)/shard_map/psum | solution.py:183
  560.0 75.1 %psum.62 = f32[]{:T(128)} all-reduce(f32[]{:T(128)} %multiply_reduce_fusion.29), channel_id=1, replica_groups=mesh['year'=8,'row'=8,'col'=4] {'year','row','col'}, use_global_device_ids=true, to_apply=%region_48.49 | all-reduce | flops 1 | bytes 8 | tf_op jit(solution)/shard_map/psum | solution.py:159
  637.9 4.0 collective-permute-start.24
  642.0 2.9 collective-permute-done.25
  645.9 3.8 collective-permute-start.27
  649.6 3.1 collective-permute-start.26
  654.7 1.5 copy.118
  656.5 1.3 collective-permute-start.29
  657.8 4.0 collective-permute-start.28
  664.3 2.0 multiply_reduce_fusion.28
  666.3 76.8 %psum.63 = f32[]{:T(128)} all-reduce(f32[]{:T(128)} %get-tuple-element.43), channel_id=1, replica_groups=mesh['year'=8,'row'=8,'col'=4] {'year','row','col'}, use_global_device_ids=true, to_apply=%region_50.51 | all-reduce | flops 1 | bytes 8 | tf_op jit(solution)/shard_map/psum | solution.py:183
  (532 shorter events, 62.9 us)
Async XLA Ops:
  0.6 36.9 %collective-permute-start.1 = (f32[1,7,64,128]{3,2,1,0:T(8,128)}, f32[1,7,64,128]{3,2,1,0:T(8,128)S(1)}, u32[]{:S(2)}, u32[]{:S(2)}) collective-permute-start(f32[1,7,64,128]{3,2,1,0:T(8,128)} %param.9), channel_id=1, source_target_pairs={{32,0},{64,32},{96,64},{128,96},{160,128},{192,160},{224,192},{33,... | collective-permute-start | bytes 688136 | tf_op jit(solution)/shard_map/ppermute | solution.py:22
  1.9 35.5 %collective-permute-start = (f32[1,7,64,128]{3,2,1,0:T(8,128)}, f32[1,7,64,128]{3,2,1,0:T(8,128)S(1)}, u32[]{:S(2)}, u32[]{:S(2)}) collective-permute-start(f32[1,7,64,128]{3,2,1,0:T(8,128)} %param.9), channel_id=1, source_target_pairs={{0,32},{32,64},{64,96},{96,128},{128,160},{160,192},{192,224},{1,3... | collective-permute-start | bytes 688136 | tf_op jit(solution)/shard_map/ppermute | solution.py:20
  37.6 6.7 collective-permute-start.3
  42.3 3.1 collective-permute-start.2
  48.4 6.5 collective-permute-start.5
  49.7 4.8 collective-permute-start.4
  62.2 7.7 %collective-permute-start.7 = (f32[1,7,64,128]{3,2,1,0:T(8,128)S(1)}, f32[1,7,64,128]{3,2,1,0:T(8,128)S(1)}, u32[]{:S(2)}, u32[]{:S(2)}) collective-permute-start(f32[1,7,64,128]{3,2,1,0:T(8,128)S(1)} %constant_dynamic-update-slice_fusion.10), channel_id=1, source_target_pairs={{32,0},{64,32},{96,64},{128,96},{160,128},{192,160},{224,192},{33,... | collective-permute-start | bytes 688136 | tf_op jit(solution)/shard_map/ppermute | solution.py:22
  63.4 7.3 collective-permute-start.6
  70.8 7.7 %collective-permute-start.9 = (f32[3,7,1,128]{3,1,2,0:T(8,128)S(1)}, f32[3,7,1,128]{3,1,2,0:T(8,128)S(1)}, u32[]{:S(2)}, u32[]{:S(2)}) collective-permute-start(f32[3,7,1,128]{3,1,2,0:T(8,128)S(1)} %copy.125), channel_id=1, source_target_pairs={{4,0},{8,4},{12,8},{16,12},{20,16},{24,20},{28,24},{5,1},{9,5},{13... | collective-permute-start | bytes 32264 | tf_op jit(solution)/shard_map/ppermute | solution.py:22
  75.2 4.1 collective-permute-start.8
  81.2 5.5 collective-permute-start.10
  85.5 4.6 collective-permute-start.11
  93.9 86.5 %copy-start.107 = (f32[1,1,64,128]{3,2,1,0:T(8,128)S(1)}, f32[1,1,64,128]{3,2,1,0:T(8,128)}, u32[]{:S(2)}) copy-start(f32[1,1,64,128]{3,2,1,0:T(8,128)} %get-tuple-element.80) | copy-start | bytes 98308
  93.9 86.5 %copy-start.109 = (f32[1,1,64,128]{3,2,1,0:T(8,128)S(1)}, f32[1,1,64,128]{3,2,1,0:T(8,128)}, u32[]{:S(2)}) copy-start(f32[1,1,64,128]{3,2,1,0:T(8,128)} %get-tuple-element.81) | copy-start | bytes 98308
  93.9 86.5 %copy-start.111 = (f32[1,1,64,128]{3,2,1,0:T(8,128)S(1)}, f32[1,1,64,128]{3,2,1,0:T(8,128)}, u32[]{:S(2)}) copy-start(f32[1,1,64,128]{3,2,1,0:T(8,128)} %get-tuple-element.82) | copy-start | bytes 98308
  93.9 86.5 %copy-start.113 = (f32[1,1,64,128]{3,2,1,0:T(8,128)S(1)}, f32[1,1,64,128]{3,2,1,0:T(8,128)}, u32[]{:S(2)}) copy-start(f32[1,1,64,128]{3,2,1,0:T(8,128)} %get-tuple-element.83) | copy-start | bytes 98308
  93.9 86.5 %copy-start.78 = (f32[1,1,64,128]{3,2,1,0:T(8,128)S(1)}, f32[1,1,64,128]{3,2,1,0:T(8,128)}, u32[]{:S(2)}) copy-start(f32[1,1,64,128]{3,2,1,0:T(8,128)} %get-tuple-element.69) | copy-start | bytes 98308
  93.9 86.5 %copy-start.81 = (f32[1,1,64,128]{3,2,1,0:T(8,128)S(1)}, f32[1,1,64,128]{3,2,1,0:T(8,128)}, u32[]{:S(2)}) copy-start(f32[1,1,64,128]{3,2,1,0:T(8,128)} %get-tuple-element.70) | copy-start | bytes 98308
  93.9 86.5 %copy-start.84 = (f32[1,1,64,128]{3,2,1,0:T(8,128)S(1)}, f32[1,1,64,128]{3,2,1,0:T(8,128)}, u32[]{:S(2)}) copy-start(f32[1,1,64,128]{3,2,1,0:T(8,128)} %get-tuple-element.71) | copy-start | bytes 98308
  94.0 86.5 %copy-start.87 = (f32[1,1,64,128]{3,2,1,0:T(8,128)S(1)}, f32[1,1,64,128]{3,2,1,0:T(8,128)}, u32[]{:S(2)}) copy-start(f32[1,1,64,128]{3,2,1,0:T(8,128)} %get-tuple-element.72) | copy-start | bytes 98308
  94.0 86.5 %copy-start.90 = (f32[1,1,64,128]{3,2,1,0:T(8,128)S(1)}, f32[1,1,64,128]{3,2,1,0:T(8,128)}, u32[]{:S(2)}) copy-start(f32[1,1,64,128]{3,2,1,0:T(8,128)} %get-tuple-element.73) | copy-start | bytes 98308
  94.0 86.5 %copy-start.93 = (f32[1,1,64,128]{3,2,1,0:T(8,128)S(1)}, f32[1,1,64,128]{3,2,1,0:T(8,128)}, u32[]{:S(2)}) copy-start(f32[1,1,64,128]{3,2,1,0:T(8,128)} %get-tuple-element.74) | copy-start | bytes 98308
  94.0 86.5 %copy-start.96 = (f32[1,1,64,128]{3,2,1,0:T(8,128)S(1)}, f32[1,1,64,128]{3,2,1,0:T(8,128)}, u32[]{:S(2)}) copy-start(f32[1,1,64,128]{3,2,1,0:T(8,128)} %get-tuple-element.75) | copy-start | bytes 98308
  94.0 86.6 %copy-start.57 = (f32[1,1,64,128]{3,2,1,0:T(8,128)S(1)}, f32[1,1,64,128]{3,2,1,0:T(8,128)}, u32[]{:S(2)}) copy-start(f32[1,1,64,128]{3,2,1,0:T(8,128)} %get-tuple-element.61) | copy-start | bytes 98308
  94.0 86.6 %copy-start.60 = (f32[1,1,64,128]{3,2,1,0:T(8,128)S(1)}, f32[1,1,64,128]{3,2,1,0:T(8,128)}, u32[]{:S(2)}) copy-start(f32[1,1,64,128]{3,2,1,0:T(8,128)} %get-tuple-element.62) | copy-start | bytes 98308
  94.0 86.6 %copy-start.63 = (f32[1,1,64,128]{3,2,1,0:T(8,128)S(1)}, f32[1,1,64,128]{3,2,1,0:T(8,128)}, u32[]{:S(2)}) copy-start(f32[1,1,64,128]{3,2,1,0:T(8,128)} %get-tuple-element.63) | copy-start | bytes 98308
  94.0 86.6 %copy-start.66 = (f32[1,1,64,128]{3,2,1,0:T(8,128)S(1)}, f32[1,1,64,128]{3,2,1,0:T(8,128)}, u32[]{:S(2)}) copy-start(f32[1,1,64,128]{3,2,1,0:T(8,128)} %get-tuple-element.64) | copy-start | bytes 98308
  94.0 86.6 %copy-start.69 = (f32[1,1,64,128]{3,2,1,0:T(8,128)S(1)}, f32[1,1,64,128]{3,2,1,0:T(8,128)}, u32[]{:S(2)}) copy-start(f32[1,1,64,128]{3,2,1,0:T(8,128)} %get-tuple-element.65) | copy-start | bytes 98308
  94.0 86.6 %copy-start.72 = (f32[1,1,64,128]{3,2,1,0:T(8,128)S(1)}, f32[1,1,64,128]{3,2,1,0:T(8,128)}, u32[]{:S(2)}) copy-start(f32[1,1,64,128]{3,2,1,0:T(8,128)} %get-tuple-element.66) | copy-start | bytes 98308
  94.1 86.6 %copy-start.75 = (f32[1,1,64,128]{3,2,1,0:T(8,128)S(1)}, f32[1,1,64,128]{3,2,1,0:T(8,128)}, u32[]{:S(2)}) copy-start(f32[1,1,64,128]{3,2,1,0:T(8,128)} %get-tuple-element.67) | copy-start | bytes 98308
  256.7 8.4 %collective-permute-start.13 = (f32[1,7,64,128]{3,2,1,0:T(8,128)S(1)}, f32[1,7,64,128]{3,2,1,0:T(8,128)S(1)}, u32[]{:S(2)}, u32[]{:S(2)}) collective-permute-start(f32[1,7,64,128]{3,2,1,0:T(8,128)S(1)} %multiply_add_fusion.2), channel_id=1, source_target_pairs={{32,0},{64,32},{96,64},{128,96},{160,128},{192,160},{224,192},{33,... | collective-permute-start | bytes 688136 | tf_op jit(solution)/shard_map/ppermute | solution.py:22
  258.0 7.9 %collective-permute-start.12 = (f32[1,7,64,128]{3,2,1,0:T(8,128)S(1)}, f32[1,7,64,128]{3,2,1,0:T(8,128)S(1)}, u32[]{:S(2)}, u32[]{:S(2)}) collective-permute-start(f32[1,7,64,128]{3,2,1,0:T(8,128)S(1)} %multiply_add_fusion.2), channel_id=1, source_target_pairs={{0,32},{32,64},{64,96},{96,128},{128,160},{160,192},{192,224},{1,3... | collective-permute-start | bytes 688136 | tf_op jit(solution)/shard_map/ppermute | solution.py:20
  266.0 5.9 collective-permute-start.15
  269.8 3.1 collective-permute-start.14
  275.1 7.1 collective-permute-start.17
  276.4 5.4 collective-permute-start.16
  445.0 8.4 %collective-permute-start.19 = (f32[1,7,64,128]{3,2,1,0:T(8,128)S(1)}, f32[1,7,64,128]{3,2,1,0:T(8,128)S(1)}, u32[]{:S(2)}, u32[]{:S(2)}) collective-permute-start(f32[1,7,64,128]{3,2,1,0:T(8,128)S(1)} %multiply_add_fusion.1), channel_id=1, source_target_pairs={{32,0},{64,32},{96,64},{128,96},{160,128},{192,160},{224,192},{33,... | collective-permute-start | bytes 688136 | tf_op jit(solution)/shard_map/ppermute | solution.py:22
  446.3 7.9 %collective-permute-start.18 = (f32[1,7,64,128]{3,2,1,0:T(8,128)S(1)}, f32[1,7,64,128]{3,2,1,0:T(8,128)S(1)}, u32[]{:S(2)}, u32[]{:S(2)}) collective-permute-start(f32[1,7,64,128]{3,2,1,0:T(8,128)S(1)} %multiply_add_fusion.1), channel_id=1, source_target_pairs={{0,32},{32,64},{64,96},{96,128},{128,160},{160,192},{192,224},{1,3... | collective-permute-start | bytes 688136 | tf_op jit(solution)/shard_map/ppermute | solution.py:20
  454.3 6.3 collective-permute-start.21
  458.0 3.4 collective-permute-start.20
  466.2 7.4 collective-permute-start.23
  467.4 5.0 collective-permute-start.22
  636.6 8.4 %collective-permute-start.25 = (f32[1,7,64,128]{3,2,1,0:T(8,128)S(1)}, f32[1,7,64,128]{3,2,1,0:T(8,128)S(1)}, u32[]{:S(2)}, u32[]{:S(2)}) collective-permute-start(f32[1,7,64,128]{3,2,1,0:T(8,128)S(1)} %multiply_add_fusion), channel_id=1, source_target_pairs={{32,0},{64,32},{96,64},{128,96},{160,128},{192,160},{224,192},{33,... | collective-permute-start | bytes 688136 | tf_op jit(solution)/shard_map/ppermute | solution.py:22
  637.9 7.9 %collective-permute-start.24 = (f32[1,7,64,128]{3,2,1,0:T(8,128)S(1)}, f32[1,7,64,128]{3,2,1,0:T(8,128)S(1)}, u32[]{:S(2)}, u32[]{:S(2)}) collective-permute-start(f32[1,7,64,128]{3,2,1,0:T(8,128)S(1)} %multiply_add_fusion), channel_id=1, source_target_pairs={{0,32},{32,64},{64,96},{96,128},{128,160},{160,192},{192,224},{1,3... | collective-permute-start | bytes 688136 | tf_op jit(solution)/shard_map/ppermute | solution.py:20
  645.9 6.9 collective-permute-start.27
  649.6 3.7 collective-permute-start.26
  656.5 6.5 collective-permute-start.29
  657.8 4.8 collective-permute-start.28
  (161 other events, 3861.7 us)
where the time goes:
time: 749 us; the launch traced here: 746 us
  blocking collectives  536 us (72%)
  starting transfers between devices  87.6 us (12%)
  other arithmetic  45.2 us (6%)
  local copies, waits for them, and re-layouts  31 us (4%)
  waiting for transfers between devices  23.5 us (3%)
  between operations  22.1 us (3%)
    psum x4, blocking collectives, inner_total(): return lax.psum(jnp.sum(left_field * right_field), ('year', 'row', 'col'))  306 us
    psum x3, blocking collectives, per_device(): lax.psum(jnp.sum(direction * image), ('year', 'row', 'col'))  230 us
    ppermute x15, starting transfers between devices, with_halo(): lax.ppermute(tail, axis, [(i, (i + 1) % count) for i in range(ends)])  54.3 us
    ppermute x15, starting transfers between devices, with_halo(): lax.ppermute(head, axis, [((i + 1) % count, i) for i in range(ends)])  33.3 us
  transfers between devices with their start and end apart: 30, of which 17 were waited for; matrix products, arithmetic and copies ran while one was open for 3% of the time, Pallas kernels for 0%

commit v1 on v0

v1 whole, which is shorter than its diff:
```python
import functools

import jax
import jax.numpy as jnp
from jax import lax
from jax.experimental import pallas as pl
from jax.experimental.pallas import tpu as pltpu
from jax.sharding import PartitionSpec as P

damping = 0.1
COUNT = 7
PAIRS = [(i, j) for i in range(COUNT) for j in range(i, COUNT)]
SPOT = {}
for _n, (_i, _j) in enumerate(PAIRS):
    SPOT[_i, _j] = _n
    SPOT[_j, _i] = _n
SUB = 8
VMEM = pl.BlockSpec(memory_space=pltpu.VMEM)
SMEM = pl.BlockSpec(memory_space=pltpu.SMEM)


def blocks_kernel(num_dates, sw, tw, observed, quality, land, params, minv, grad):
    base, peak, slope, rise_mid, rise_log, fall_mid, fall_log = [params[0, k] for k in range(COUNT)]
    rise = jnp.exp(rise_log)
    fall = jnp.exp(fall_log)
    rise_half = 0.5 * rise
    fall_half = 0.5 * fall
    rise_off = rise_half * rise_mid
    fall_off = fall_half * fall_mid
    peak_half = 0.5 * peak
    slope_half = 0.5 * slope

    def date(d, sums):
        sums = list(sums)
        t = d.astype(jnp.float32) * (1.0 / num_dates)
        flag = quality[0, d]
        w = jnp.where(flag == 0, 1.0, jnp.where(flag == 1, 0.5, 0.0))
        x1 = rise_half * t - rise_off
        x2 = fall_half * t - fall_off
        th1 = jnp.tanh(x1)
        th2 = jnp.tanh(x2)
        q = th1 - th2
        m = peak_half - slope_half * t
        mis = base + m * q - observed[0, d]
        a = m - m * (th1 * th1)
        b = m - m * (th2 * th2)
        cols = [None, q, q * t, a, a * x1, b, b * x2]
        for i in range(COUNT):
            wc = w if i == 0 else w * cols[i]
            for j in range(i, COUNT):
                n = SPOT[i, j]
                sums[n] = sums[n] + (wc if j == 0 else wc * cols[j])
            sums[len(PAIRS) + i] = sums[len(PAIRS) + i] + wc * mis
        return tuple(sums)

    zero = jnp.zeros_like(base)
    sums = lax.fori_loop(0, num_dates, date, (zero,) * (len(PAIRS) + COUNT), unroll=2)
    share = land[...].astype(jnp.float32) * (1.0 / num_dates)
    scale = [None, 0.5, -0.5, -0.5 * rise, 1.0, 0.5 * fall, -1.0]
    left = [share if s is None else share * s for s in scale]
    block = {}
    for n, (i, j) in enumerate(PAIRS):
        e = sums[n] * left[i]
        if scale[j] is not None:
            e = e * scale[j]
        if i == j:
            e = e + (damping + 4.0 * sw[i] + 2.0 * tw[i])
        block[i, j] = e
    for i in range(COUNT):
        grad[i] = sums[len(PAIRS) + i] * left[i]
    key = lambda i, j: (i, j) if i <= j else (j, i)
    for k in range(COUNT):
        inv = 1.0 / block[k, k]
        row = {i: block[key(i, k)] for i in range(COUNT) if i != k}
        fac = {i: row[i] * inv for i in row}
        for i in row:
            for j in row:
                if i <= j:
                    block[i, j] = block[i, j] - fac[i] * row[j]
        for i in row:
            block[key(i, k)] = fac[i]
        block[k, k] = -inv
    for n, (i, j) in enumerate(PAIRS):
        minv[n] = -block[i, j]


def put_faces(v, row_low, row_high, col_low, col_high):
    rows, cols = v.shape[1], v.shape[2]
    lane = lax.broadcasted_iota(jnp.int32, (rows, cols), 1)
    low = jnp.zeros((rows, cols), jnp.float32)
    high = low
    for p in range(COUNT):
        row_low[p : p + 1] = v[p, 0:1]
        row_high[p : p + 1] = v[p, rows - 1 : rows]
        low = jnp.where(lane == p, v[p, :, 0:1], low)
        high = jnp.where(lane == p, v[p, :, cols - 1 : cols], high)
    row_low[COUNT : COUNT + 1] = jnp.zeros((1, cols), jnp.float32)
    row_high[COUNT : COUNT + 1] = jnp.zeros((1, cols), jnp.float32)
    col_low[...] = low
    col_high[...] = high


def faces_kernel(v, *faces):
    put_faces(v, *faces)


def low_sides(x, p, ends, ylo, rlo, clo):
    rows, cols = x.shape
    row = lax.broadcasted_iota(jnp.int32, x.shape, 0)
    lane = lax.broadcasted_iota(jnp.int32, x.shape, 1)
    yl = jnp.where(ends[0] == 1, x, ylo[p])
    face = jnp.where(ends[2] == 1, x[0:1], rlo[p : p + 1])
    rl = jnp.where(row == 0, face, pltpu.roll(x, 1, 0))
    face = jnp.where(ends[4] == 1, x[:, 0:1], clo[:, p : p + 1])
    cl = jnp.where(lane == 0, face, pltpu.roll(x, 1, 1))
    return yl, rl, cl


def high_sides(x, p, ends, yhi, rhi, chi):
    rows, cols = x.shape
    row = lax.broadcasted_iota(jnp.int32, x.shape, 0)
    lane = lax.broadcasted_iota(jnp.int32, x.shape, 1)
    yh = jnp.where(ends[1] == 1, x, yhi[p])
    face = jnp.where(ends[3] == 1, x[rows - 1 : rows], rhi[p : p + 1])
    rh = jnp.where(row == rows - 1, face, pltpu.roll(x, rows - 1, 0))
    face = jnp.where(ends[5] == 1, x[:, cols - 1 : cols], chi[:, p : p + 1])
    ch = jnp.where(lane == cols - 1, face, pltpu.roll(x, cols - 1, 1))
    return yh, rh, ch


def side_sums(x, p, ends, halo):
    ylo, rlo, clo, yhi, rhi, chi = halo
    yl, rl, cl = low_sides(x, p, ends, ylo, rlo, clo)
    yh, rh, ch = high_sides(x, p, ends, yhi, rhi, chi)
    return rl + rh + cl + ch, yl + yh


def solve_blocks(minv, u, v, dots, last=None):
    rows = u.shape[1]
    even = jnp.zeros((SUB, u.shape[2]), jnp.float32)
    odd = even
    for c in range(rows // SUB):
        at = slice(c * SUB, (c + 1) * SUB)
        us = [u[p, at] for p in range(COUNT)]
        for i in range(COUNT):
            total = minv[SPOT[i, 0], at] * us[0]
            for j in range(1, COUNT):
                total = total + minv[SPOT[i, j], at] * us[j]
            v[i, at] = total
            even = even + total * us[i]
            if last is not None:
                odd = odd + last[i, at] * us[i]
    dots[0] = even
    dots[1] = odd


def first_kernel(ends, sw, tw, minv, grad, params, *refs):
    halo, (u, v, dots), faces = refs[:6], refs[6:9], refs[9:]
    for p in range(COUNT):
        x = params[p]
        plane, yearly = side_sums(x, p, ends, halo)
        u[p] = -(grad[p] + (sw[p] * (4.0 * x - plane) + tw[p] * (2.0 * x - yearly)))
    solve_blocks(minv, u, v, dots)
    put_faces(v, *faces)


def next_kernel(ends, sw, tw, minv, last, *refs):
    halo, (u, v, dots), faces = refs[:6], refs[6:9], refs[9:]
    for p in range(COUNT):
        plane, yearly = side_sums(last[p], p, ends, halo)
        u[p] = sw[p] * plane + tw[p] * yearly
    solve_blocks(minv, u, v, dots, last)
    put_faces(v, *faces)


def moments_kernel(ends, sw, tw, v, ylo, rlo, clo, dots0, dots1, dots2, dots3, sums):
    rows, cols = v.shape[1], v.shape[2]
    row = lax.broadcasted_iota(jnp.int32, (rows, cols), 0)
    lane = lax.broadcasted_iota(jnp.int32, (rows, cols), 1)
    end = [ends[n].astype(jnp.float32) for n in range(6)]
    edge = jnp.where(row == rows - 1, end[3], 0.0) - jnp.where(row == 0, end[2], 0.0)
    edge = edge + jnp.where(lane == cols - 1, end[5], 0.0) - jnp.where(lane == 0, end[4], 0.0)
    total = jnp.zeros((rows, cols), jnp.float32)
    for p in range(COUNT):
        x = v[p]
        yl, rl, cl = low_sides(x, p, ends, ylo, rlo, clo)
        plane = 2.0 * (rl + cl) + edge * x
        yearly = 2.0 * yl + (end[1] - end[0]) * x
        total = total + x * (sw[p] * plane + tw[p] * yearly)
    last = total[0:SUB]
    for c in range(1, rows // SUB):
        last = last + total[c * SUB : (c + 1) * SUB]
    parts = [dots0[0], dots1[1], dots1[0], dots2[1], dots2[0], dots3[1], dots3[0], last]
    high = jnp.concatenate([jnp.sum(part, axis=0, keepdims=True) for part in parts], axis=0)
    high = jnp.sum(high, axis=1, keepdims=True)
    row = lax.broadcasted_iota(jnp.int32, (SUB, cols), 0)
    lane = lax.broadcasted_iota(jnp.int32, (SUB, cols), 1)
    line = jnp.sum(jnp.where(row == lane, high, 0.0), axis=0, keepdims=True)
    sums[...] = jnp.broadcast_to(line, sums.shape)


def solve4(gram, right):
    n = len(right)
    low = [[None] * n for _ in range(n)]
    diag = [None] * n
    for j in range(n):
        diag[j] = gram[j][j]
        for k in range(j):
            diag[j] = diag[j] - low[j][k] * low[j][k] * diag[k]
        for i in range(j + 1, n):
            e = gram[i][j]
            for k in range(j):
                e = e - low[i][k] * low[j][k] * diag[k]
            low[i][j] = e / diag[j]
    y = []
    for i in range(n):
        e = right[i]
        for k in range(i):
            e = e - low[i][k] * y[k]
        y.append(e)
    y = [y[i] / diag[i] for i in range(n)]
    for i in reversed(range(n)):
        for k in range(i + 1, n):
            y[i] = y[i] - low[k][i] * y[k]
    return y


def last_kernel(ends, sw, tw, sums, params, *refs):
    us, vs, halo, (new_params, residual) = refs[:4], refs[4:8], refs[8:14], refs[14:]
    rows, cols = params.shape[1], params.shape[2]
    line = jnp.sum(sums[...], axis=0, keepdims=True)
    lane = lax.broadcasted_iota(jnp.int32, line.shape, 1)
    mom = [jnp.sum(jnp.where(lane == n, line, 0.0), axis=1, keepdims=True) for n in range(8)]
    gram = [[mom[i + j] - mom[i + j + 1] for j in range(4)] for i in range(4)]
    y = [jnp.broadcast_to(e, (SUB, cols)) for e in solve4(gram, mom[:4])]
    y = [jnp.concatenate([e] * (rows // SUB), axis=0) for e in y]
    for p in range(COUNT):
        plane, yearly = side_sums(vs[3][p], p, ends, halo)
        new = sw[p] * plane + tw[p] * yearly
        step = y[0] * vs[0][p]
        for k in range(1, 4):
            step = step + y[k] * vs[k][p]
        new_params[p] = params[p] + step
        chain = [us[k][p] for k in range(4)] + [new]
        left = chain[0]
        for k in range(4):
            left = left - y[k] * (chain[k] - chain[k + 1])
        residual[p] = left


def call(kernel, out_shape, name, num_smem, args):
    return pl.pallas_call(
        kernel,
        out_shape=[jax.ShapeDtypeStruct(s, jnp.float32) for s in out_shape],
        in_specs=[SMEM] * num_smem + [VMEM] * (len(args) - num_smem),
        out_specs=[VMEM] * len(out_shape),
        compiler_params=pltpu.CompilerParams(vmem_limit_bytes=24 * 1024 * 1024),
        name=name,
    )(*args)


def ring(axis, shift):
    count = lax.axis_size(axis)
    return [(i, (i + shift) % count) for i in range(count)]


def exchange(v, faces):
    row_low, row_high, col_low, col_high = faces
    return (
        lax.ppermute(v, "year", ring("year", 1)),
        lax.ppermute(row_high, "row", ring("row", 1)),
        lax.ppermute(col_high, "col", ring("col", 1)),
        lax.ppermute(v, "year", ring("year", -1)),
        lax.ppermute(row_low, "row", ring("row", -1)),
        lax.ppermute(col_low, "col", ring("col", -1)),
    )


def per_device(observed, quality, land_mask, params, spatial_weight, temporal_weight):
    num_dates, rows, cols = observed.shape[1:]
    axes = ("year", "row", "col")
    devices = lax.axis_size(axes)
    ends = []
    for axis in axes:
        here = lax.axis_index(axis)
        ends += [here == 0, here == lax.axis_size(axis) - 1]
    ends = jnp.stack(ends).astype(jnp.int32)
    small = (ends, spatial_weight, temporal_weight)

    field = (COUNT, rows, cols)
    faces = [(SUB, cols)] * 2 + [(rows, cols)] * 2
    dots = (2, SUB, cols)
    current = params.reshape(field)
    halo = exchange(current, call(faces_kernel, faces, "faces", 0, (current,)))

    strip = lambda lead: pl.BlockSpec(lead + (SUB, cols), lambda i: (0,) * len(lead) + (i, 0))
    minv, grad = pl.pallas_call(
        functools.partial(blocks_kernel, num_dates),
        grid=(rows // SUB,),
        out_shape=[
            jax.ShapeDtypeStruct((len(PAIRS), rows, cols), jnp.float32),
            jax.ShapeDtypeStruct(field, jnp.float32),
        ],
        in_specs=[SMEM, SMEM, strip((1, num_dates)), strip((1, num_dates)), strip(()), strip((1, COUNT))],
        out_specs=[strip((len(PAIRS),)), strip((COUNT,))],
        compiler_params=pltpu.CompilerParams(vmem_limit_bytes=24 * 1024 * 1024),
        cost_estimate=pl.CostEstimate(flops=60000000, bytes_accessed=5000000, transcendentals=800000),
        name="blocks",
    )(spatial_weight, temporal_weight, observed, quality, land_mask, params)

    step_out = [field, field, dots] + faces
    u, v, dot, *face = call(
        first_kernel, step_out, "first", 3, small + (minv, grad, current) + halo
    )
    us, vs, ds = [u], [v], [dot]
    for _ in range(3):
        halo = exchange(v, face)
        u, v, dot, *face = call(next_kernel, step_out, "next", 3, small + (minv, v) + halo)
        us.append(u)
        vs.append(v)
        ds.append(dot)
    halo = exchange(v, face)
    (sums,) = call(
        moments_kernel, [(devices, cols)], "moments", 3, small + (v,) + halo[:3] + tuple(ds)
    )
    sums = lax.all_to_all(sums, axes, 0, 0, tiled=True)
    new_params, residual = call(
        last_kernel, [field, field], "last", 3, small + (sums, current) + tuple(us) + tuple(vs) + halo
    )
    return (new_params.reshape(params.shape), residual.reshape(params.shape))


def solution(mesh):
    field = P("year", None, "row", "col")
    return jax.shard_map(
        per_device,
        mesh=mesh,
        in_specs=(field, field, P("row", "col"), field, P(), P()),
        out_specs=(field, field),
        check_vma=False,
    )
```

time: 749 us -> 108 us (0.14)
  blocking collectives: 536 us -> 0 us
  other arithmetic: 45.2 us -> 0.01 us
  starting transfers between devices: 87.6 us -> 57.2 us
  local copies, waits for them, and re-layouts: 31 us -> 6.9 us
  Pallas kernels: 0 us -> 21.8 us
  between operations: 22.1 us -> 0.83 us
    psum x7 -> x0, blocking collectives: 536 us -> none  [the longest x4 306 us: inner_total(): return lax.psum(jnp.sum(left_field * right_field), ('year', 'row', 'col'))]
    ppermute x30, starting transfers between devices: 87.6 us -> 51.2 us  [the longest x5 20.1 us: exchange(): lax.ppermute(v, 'year', ring('year', -1))]
    pallas_call x0 -> x8, Pallas kernels: none -> 21.8 us  [the longest x7 11.9 us: call(): pl.pallas_call(kernel, out_shape=[jax.ShapeDtypeStruct(s, jnp.float32) fo...]
    reduce_sum x8 -> x0, other arithmetic: 19.5 us -> none  [the longest x4 9.69 us: per_device(): jnp.sum(direction * image)]
    slice x18 -> x0, local copies, waits for them, and re-layouts: 16.3 us -> none  [the longest x11 10.9 us: with_halo(): lax.slice_in_dim(cells, cells.shape[dim] - width, cells.shape[dim], axis=...]
    unnamed x42 -> x0, other arithmetic: 9.95 us -> none
    ppermute x20 -> x0, local copies, waits for them, and re-layouts: 9.36 us -> none  [the longest x10 6.66 us: with_halo(): lax.ppermute(head, axis, [((i + 1) % count, i) for i in range(ends)])]
  transfers between devices with their start and end apart: 30 -> 31, of which waited for: 17 -> 12; matrix products, arithmetic and copies ran while one was open for 3% -> 0% of each run, Pallas kernels for 0% -> 9%
where the time goes in v1:
time: 108 us
  starting transfers between devices  57.2 us (53%)
  Pallas kernels  21.8 us (20%)
  waiting for transfers between devices  20.9 us (19%)
  local copies, waits for them, and re-layouts  6.9 us (6%)
    ppermute x5, starting transfers between devices, exchange(): lax.ppermute(v, 'year', ring('year', -1))  20.1 us
    ppermute x5, starting transfers between devices, exchange(): lax.ppermute(row_low, 'row', ring('row', -1))  14.1 us
    ppermute x5, starting transfers between devices, exchange(): lax.ppermute(col_low, 'col', ring('col', -1))  12.1 us
    pallas_call x7, Pallas kernels, call(): pl.pallas_call(kernel, out_shape=[jax.ShapeDtypeStruct(s, jnp.float32) fo...  11.9 us
    pallas_call x1, Pallas kernels, per_device(): pl.pallas_call(functools.partial(blocks_kernel, num_dates), grid=(rows //...  9.89 us
    unnamed x20, local copies, waits for them, and re-layouts  6.8 us
    ppermute x5, waiting for transfers between devices, exchange(): lax.ppermute(row_high, 'row', ring('row', 1))  6.46 us
    all_to_all x1, starting transfers between devices, per_device(): sums = lax.all_to_all(sums, axes, 0, 0, tiled=True)  6.05 us
  transfers between devices with their start and end apart: 31, of which 12 were waited for; matrix products, arithmetic and copies ran while one was open for 0% of the time, Pallas kernels for 9%

profile of v1, /device:TPU:1, one launch (start us, length us, event | category | flops | bytes accessed | tf_op | source)
XLA Modules:
  0.0 107.7 jit_solution(17591261087184824477)
XLA Ops:
  0.6 6.5 %collective-permute-start.3 = (f32[7,64,128]{2,1,0:T(8,128)}, f32[7,64,128]{2,1,0:T(8,128)S(1)}, u32[]{:S(2)}, u32[]{:S(2)}) collective-permute-start(f32[7,64,128]{2,1,0:T(8,128)} %bitcast.13), channel_id=1, source_target_pairs={{0,224},{32,0},{64,32},{96,64},{128,96},{160,128},{192,160},{224,1... | collective-permute-start | bytes 688136 | tf_op jit(solution)/shard_map/ppermute | solution.py:273
  7.1 1.0 copy-done
  8.1 0.2 faces.1
  8.3 1.4 %collective-permute-start.2 = (f32[64,128]{1,0:T(8,128)S(1)}, f32[64,128]{1,0:T(8,128)S(1)}, u32[]{:S(2)}, u32[]{:S(2)}) collective-permute-start(f32[64,128]{1,0:T(8,128)S(1)} %get-tuple-element.41), channel_id=1, source_target_pairs={{0,1},{1,2},{2,3},{3,0},{4,5},{5,6},{6,7},{7,4},{8,9},{9,10},{10,1... | collective-permute-start | bytes 98312 | tf_op jit(solution)/shard_map/ppermute | solution.py:272
  9.7 1.5 %collective-permute-start.5 = (f32[64,128]{1,0:T(8,128)S(1)}, f32[64,128]{1,0:T(8,128)S(1)}, u32[]{:S(2)}, u32[]{:S(2)}) collective-permute-start(f32[64,128]{1,0:T(8,128)S(1)} %get-tuple-element.43), channel_id=1, source_target_pairs={{0,3},{1,0},{2,1},{3,2},{4,7},{5,4},{6,5},{7,6},{8,11},{9,8},{10,9... | collective-permute-start | bytes 98312 | tf_op jit(solution)/shard_map/ppermute | solution.py:275
  11.2 2.5 %collective-permute-start.1 = (f32[8,128]{1,0:T(8,128)S(1)}, f32[8,128]{1,0:T(8,128)S(1)}, u32[]{:S(2)}, u32[]{:S(2)}) collective-permute-start(f32[8,128]{1,0:T(8,128)S(1)} %get-tuple-element.40), channel_id=1, source_target_pairs={{0,4},{4,8},{8,12},{12,16},{16,20},{20,24},{24,28},{28,0},{1,5},{5... | collective-permute-start | bytes 12296 | tf_op jit(solution)/shard_map/ppermute | solution.py:271
  13.7 0.1 stack.27
  13.8 0.6 collective-permute-done.1.refs_1_
  14.4 2.4 %collective-permute-start.4 = (f32[8,128]{1,0:T(8,128)S(1)}, f32[8,128]{1,0:T(8,128)S(1)}, u32[]{:S(2)}, u32[]{:S(2)}) collective-permute-start(f32[8,128]{1,0:T(8,128)S(1)} %get-tuple-element.42), channel_id=1, source_target_pairs={{0,28},{4,0},{8,4},{12,8},{16,12},{20,16},{24,20},{28,24},{1,29},{... | collective-permute-start | bytes 12296 | tf_op jit(solution)/shard_map/ppermute | solution.py:274
  16.8 0.9 copy-done.1
  17.8 1.4 %copy-done.3 = f32[1,46,64,128]{3,2,1,0:T(8,128)S(1)} copy-done((f32[1,46,64,128]{3,2,1,0:T(8,128)S(1)}, f32[1,46,64,128]{3,2,1,0:T(8,128)}, u32[]{:S(2)}) %copy-start.3) | copy-done | bytes 1507352
  19.2 1.4 %copy-done.4 = s32[1,46,64,128]{3,2,1,0:T(8,128)S(1)} copy-done((s32[1,46,64,128]{3,2,1,0:T(8,128)S(1)}, s32[1,46,64,128]{3,2,1,0:T(8,128)}, u32[]{:S(2)}) %copy-start.4) | copy-done | bytes 1507352
  20.5 0.8 copy-done.5
  21.3 0.7 copy-done.6
  22.0 0.7 copy-done.8
  22.6 9.9 %blocks.1 = (f32[28,64,128]{2,1,0:T(8,128)S(1)}, f32[7,64,128]{2,1,0:T(8,128)S(1)}) custom-call(f32[7]{0:T(128)S(1)} %copy-done.6, f32[7]{0:T(128)S(1)} %copy-done.8, f32[1,46,64,128]{3,2,1,0:T(8,128)S(1)} %copy-done.3, s32[1,46,64,128]{3,2,1,0:T(8,128)S(1)} %copy-done.4, s32[64,128]{1,0:T(8,128)S(1)} %copy-done.5, f32[1,7,64,128]{3,2,1,0:T(8,128)S(1)} %copy-done.1), custom_call_target="tpu_custom_call" | custom-call | flops 60000000 | bytes 5000000 | tf_op jit(solution)/shard_map/blocks/pallas_call | solution.py:297
  32.6 1.9 %first.1 = (f32[7,64,128]{2,1,0:T(8,128)S(1)}, f32[7,64,128]{2,1,0:T(8,128)S(1)}, f32[2,8,128]{2,1,0:T(8,128)S(1)}, f32[8,128]{1,0:T(8,128)S(1)}, f32[8,128]{1,0...) custom-call(s32[6]{0:T(128)S(1)} %convert_element_type.3.ends, f32[7]{0:T(128)S(1)} %copy-done.6, ...), custom_call_target="tpu_custom_call" | custom-call | tf_op jit(solution)/shard_map/first/pallas_call | solution.py:252
  34.5 3.0 %collective-permute-start.9 = (f32[7,64,128]{2,1,0:T(8,128)S(1)}, f32[7,64,128]{2,1,0:T(8,128)S(1)}, u32[]{:S(2)}, u32[]{:S(2)}) collective-permute-start(f32[7,64,128]{2,1,0:T(8,128)S(1)} %get-tuple-element.44.last.refs_4_), channel_id=1, source_target_pairs={{0,224},{32,0},{64,32},{96,64},{128,96},{160,128},{192,160},{224,1... | collective-permute-start | bytes 688136 | tf_op jit(solution)/shard_map/ppermute | solution.py:273
  37.6 2.6 %collective-permute-start.11 = (f32[64,128]{1,0:T(8,128)S(1)}, f32[64,128]{1,0:T(8,128)S(1)}, u32[]{:S(2)}, u32[]{:S(2)}) collective-permute-start(f32[64,128]{1,0:T(8,128)S(1)} %get-tuple-element.48), channel_id=1, source_target_pairs={{0,3},{1,0},{2,1},{3,2},{4,7},{5,4},{6,5},{7,6},{8,11},{9,8},{10,9... | collective-permute-start | bytes 98312 | tf_op jit(solution)/shard_map/ppermute | solution.py:275
  40.2 0.7 collective-permute-start.7
  40.9 0.8 collective-permute-done.7.refs_1_
  41.7 3.6 %collective-permute-start.10 = (f32[8,128]{1,0:T(8,128)S(1)}, f32[8,128]{1,0:T(8,128)S(1)}, u32[]{:S(2)}, u32[]{:S(2)}) collective-permute-start(f32[8,128]{1,0:T(8,128)S(1)} %get-tuple-element.47), channel_id=1, source_target_pairs={{0,28},{4,0},{8,4},{12,8},{16,12},{20,16},{24,20},{28,24},{1,29},{... | collective-permute-start | bytes 12296 | tf_op jit(solution)/shard_map/ppermute | solution.py:274
  45.3 0.8 collective-permute-done.10.refs_4_
  46.1 1.9 %next.3 = (f32[7,64,128]{2,1,0:T(8,128)S(1)}, f32[7,64,128]{2,1,0:T(8,128)S(1)}, f32[2,8,128]{2,1,0:T(8,128)S(1)}, f32[8,128]{1,0:T(8,128)S(1)}, f32[8,128]{1,0:...) custom-call(s32[6]{0:T(128)S(1)} %convert_element_type.3.ends, f32[7]{0:T(128)S(1)} %copy-done.6, ...), custom_call_target="tpu_custom_call" | custom-call | tf_op jit(solution)/shard_map/next/pallas_call | solution.py:252
  48.1 3.0 %collective-permute-start.15 = (f32[7,64,128]{2,1,0:T(8,128)S(1)}, f32[7,64,128]{2,1,0:T(8,128)S(1)}, u32[]{:S(2)}, u32[]{:S(2)}) collective-permute-start(f32[7,64,128]{2,1,0:T(8,128)S(1)} %get-tuple-element.49.last.refs_5_), channel_id=1, source_target_pairs={{0,224},{32,0},{64,32},{96,64},{128,96},{160,128},{192,160},{224,1... | collective-permute-start | bytes 688136 | tf_op jit(solution)/shard_map/ppermute | solution.py:273
  51.1 2.7 %collective-permute-start.17 = (f32[64,128]{1,0:T(8,128)S(1)}, f32[64,128]{1,0:T(8,128)S(1)}, u32[]{:S(2)}, u32[]{:S(2)}) collective-permute-start(f32[64,128]{1,0:T(8,128)S(1)} %get-tuple-element.53), channel_id=1, source_target_pairs={{0,3},{1,0},{2,1},{3,2},{4,7},{5,4},{6,5},{7,6},{8,11},{9,8},{10,9... | collective-permute-start | bytes 98312 | tf_op jit(solution)/shard_map/ppermute | solution.py:275
  53.8 0.1 collective-permute-start.13
  53.9 1.9 %collective-permute-done.13.refs_1_ = f32[8,128]{1,0:T(8,128)S(1)} collective-permute-done((f32[8,128]{1,0:T(8,128)S(1)}, f32[8,128]{1,0:T(8,128)S(1)}, u32[]{:S(2)}, u32[]{:S(2)}) %collective-permute-start.13) | collective-permute-done | bytes 4128 | tf_op jit(solution)/shard_map/ppermute | solution.py:271
  55.8 3.6 %collective-permute-start.16 = (f32[8,128]{1,0:T(8,128)S(1)}, f32[8,128]{1,0:T(8,128)S(1)}, u32[]{:S(2)}, u32[]{:S(2)}) collective-permute-start(f32[8,128]{1,0:T(8,128)S(1)} %get-tuple-element.52), channel_id=1, source_target_pairs={{0,28},{4,0},{8,4},{12,8},{16,12},{20,16},{24,20},{28,24},{1,29},{... | collective-permute-start | bytes 12296 | tf_op jit(solution)/shard_map/ppermute | solution.py:274
  59.4 0.8 collective-permute-done.16.refs_4_
  60.2 1.9 %next.4 = (f32[7,64,128]{2,1,0:T(8,128)S(1)}, f32[7,64,128]{2,1,0:T(8,128)S(1)}, f32[2,8,128]{2,1,0:T(8,128)S(1)}, f32[8,128]{1,0:T(8,128)S(1)}, f32[8,128]{1,0:...) custom-call(s32[6]{0:T(128)S(1)} %convert_element_type.3.ends, f32[7]{0:T(128)S(1)} %copy-done.6, ...), custom_call_target="tpu_custom_call" | custom-call | tf_op jit(solution)/shard_map/next/pallas_call | solution.py:252
  62.2 3.0 %collective-permute-start.21 = (f32[7,64,128]{2,1,0:T(8,128)S(1)}, f32[7,64,128]{2,1,0:T(8,128)S(1)}, u32[]{:S(2)}, u32[]{:S(2)}) collective-permute-start(f32[7,64,128]{2,1,0:T(8,128)S(1)} %get-tuple-element.54.last.refs_6_), channel_id=1, source_target_pairs={{0,224},{32,0},{64,32},{96,64},{128,96},{160,128},{192,160},{224,1... | collective-permute-start | bytes 688136 | tf_op jit(solution)/shard_map/ppermute | solution.py:273
  65.3 2.7 %collective-permute-start.23 = (f32[64,128]{1,0:T(8,128)S(1)}, f32[64,128]{1,0:T(8,128)S(1)}, u32[]{:S(2)}, u32[]{:S(2)}) collective-permute-start(f32[64,128]{1,0:T(8,128)S(1)} %get-tuple-element.58), channel_id=1, source_target_pairs={{0,3},{1,0},{2,1},{3,2},{4,7},{5,4},{6,5},{7,6},{8,11},{9,8},{10,9... | collective-permute-start | bytes 98312 | tf_op jit(solution)/shard_map/ppermute | solution.py:275
  67.9 2.0 %collective-permute-done.19.refs_1_ = f32[8,128]{1,0:T(8,128)S(1)} collective-permute-done((f32[8,128]{1,0:T(8,128)S(1)}, f32[8,128]{1,0:T(8,128)S(1)}, u32[]{:S(2)}, u32[]{:S(2)}) %collective-permute-start.19) | collective-permute-done | bytes 4128 | tf_op jit(solution)/shard_map/ppermute | solution.py:271
  69.9 3.6 %collective-permute-start.22 = (f32[8,128]{1,0:T(8,128)S(1)}, f32[8,128]{1,0:T(8,128)S(1)}, u32[]{:S(2)}, u32[]{:S(2)}) collective-permute-start(f32[8,128]{1,0:T(8,128)S(1)} %get-tuple-element.57), channel_id=1, source_target_pairs={{0,28},{4,0},{8,4},{12,8},{16,12},{20,16},{24,20},{28,24},{1,29},{... | collective-permute-start | bytes 12296 | tf_op jit(solution)/shard_map/ppermute | solution.py:274
  73.5 0.8 collective-permute-done.22.refs_4_
  74.4 1.9 %next.5 = (f32[7,64,128]{2,1,0:T(8,128)S(1)}, f32[7,64,128]{2,1,0:T(8,128)S(1)}, f32[2,8,128]{2,1,0:T(8,128)S(1)}, f32[8,128]{1,0:T(8,128)S(1)}, f32[8,128]{1,0:...) custom-call(s32[6]{0:T(128)S(1)} %convert_element_type.3.ends, f32[7]{0:T(128)S(1)} %copy-done.6, ...), custom_call_target="tpu_custom_call" | custom-call | tf_op jit(solution)/shard_map/next/pallas_call | solution.py:252
  76.5 1.2 %collective-permute-done.25.rlo.refs_9_ = f32[8,128]{1,0:T(8,128)S(1)} collective-permute-done((f32[8,128]{1,0:T(8,128)S(1)}, f32[8,128]{1,0:T(8,128)S(1)}, u32[]{:S(2)}, u32[]{:S(2)}) %collective-permute-start.25) | collective-permute-done | bytes 4128 | tf_op jit(solution)/shard_map/ppermute | solution.py:271
  77.7 2.8 %collective-permute-done.26.clo.refs_10_ = f32[64,128]{1,0:T(8,128)S(1)} collective-permute-done((f32[64,128]{1,0:T(8,128)S(1)}, f32[64,128]{1,0:T(8,128)S(1)}, u32[]{:S(2)}, u32[]{:S(2)}) %collective-permute-start.26) | collective-permute-done | bytes 32800 | tf_op jit(solution)/shard_map/ppermute | solution.py:272
  80.5 4.4 %collective-permute-done.24.ylo.refs_8_ = f32[7,64,128]{2,1,0:T(8,128)S(1)} collective-permute-done((f32[7,64,128]{2,1,0:T(8,128)S(1)}, f32[7,64,128]{2,1,0:T(8,128)S(1)}, u32[]{:S(2)}, u32[]{:S(2)}) %collective-permute-start.24) | collective-permute-done | bytes 229408 | tf_op jit(solution)/shard_map/ppermute | solution.py:270
  84.9 1.6 %moments.1 = f32[256,128]{1,0:T(8,128)} custom-call(s32[6]{0:T(128)S(1)} %convert_element_type.3.ends, f32[7]{0:T(128)S(1)} %copy-done.6, f32[7]{0:T(128)S(1)} %copy-done.8, f32[7,64,128]{2,1,0:T(8,128)S(1)} %get-tuple-element.59.v.refs_7_, f32[7,64,128]{2,1,0:T(8,128)S(1)} %collective-permute-done.24.ylo.refs_8_, ...), custom_call_target="tpu_custom_call" | custom-call | tf_op jit(solution)/shard_map/moments/pallas_call | solution.py:252
  86.5 6.0 %all-to-all-start = ((f32[256,1,128]{2,1,0:T(1,128)}), f32[256,1,128]{2,1,0:T(1,128)S(1)}, u32[]{:S(2)}, u32[]{:S(2)}) async-start(f32[256,1,128]{2,1,0:T(1,128)} %bitcast.8), calls=%async_computation | async-start | bytes 262144 | tf_op jit(solution)/shard_map/all_to_all | solution.py:326
  92.5 4.5 %collective-permute-start.27 = (f32[7,64,128]{2,1,0:T(8,128)S(1)}, f32[7,64,128]{2,1,0:T(8,128)S(1)}, u32[]{:S(2)}, u32[]{:S(2)}) collective-permute-start(f32[7,64,128]{2,1,0:T(8,128)S(1)} %get-tuple-element.59.v.refs_7_), channel_id=1, source_target_pairs={{0,224},{32,0},{64,32},{96,64},{128,96},{160,128},{192,160},{224,1... | collective-permute-start | bytes 688136 | tf_op jit(solution)/shard_map/ppermute | solution.py:273
  97.1 2.6 %collective-permute-start.29 = (f32[64,128]{1,0:T(8,128)S(1)}, f32[64,128]{1,0:T(8,128)S(1)}, u32[]{:S(2)}, u32[]{:S(2)}) collective-permute-start(f32[64,128]{1,0:T(8,128)S(1)} %get-tuple-element.71), channel_id=1, source_target_pairs={{0,3},{1,0},{2,1},{3,2},{4,7},{5,4},{6,5},{7,6},{8,11},{9,8},{10,9... | collective-permute-start | bytes 98312 | tf_op jit(solution)/shard_map/ppermute | solution.py:275
  99.7 0.9 collective-permute-start.28
  100.6 2.7 %collective-permute-done.28.refs_12_ = f32[8,128]{1,0:T(8,128)S(1)} collective-permute-done((f32[8,128]{1,0:T(8,128)S(1)}, f32[8,128]{1,0:T(8,128)S(1)}, u32[]{:S(2)}, u32[]{:S(2)}) %collective-permute-start.28) | collective-permute-done | bytes 4128 | tf_op jit(solution)/shard_map/ppermute | solution.py:274
  103.3 2.1 %all-to-all-done = f32[256,1,128]{2,1,0:T(1,128)S(1)} async-done(((f32[256,1,128]{2,1,0:T(1,128)}), f32[256,1,128]{2,1,0:T(1,128)S(1)}, u32[]{:S(2)}, u32[]{:S(2)}) %all-to-all-start) | async-done | bytes 131104 | tf_op jit(solution)/shard_map/all_to_all | solution.py:326
  105.4 2.3 %last.1 = (f32[7,64,128]{2,1,0:T(8,128)}, f32[7,64,128]{2,1,0:T(8,128)}) custom-call(s32[6]{0:T(128)S(1)} %convert_element_type.3.ends, f32[7]{0:T(128)S(1)} %copy-done.7, f32[7]{0:T(128)S(1)} %copy-done.9, f32[256,128]{1,0:T(8,128)S(1)} %bitcast.18, f32[7,64,128]{2,1,0:T(8,128)S(1)} %bitcast.17, f32[7,64,128]{2,1,0:T(8,128)S(1)} %get-tuple-element.66.refs_0_, ...), custom_call_target="tpu_custom_call" | custom-call | tf_op jit(solution)/shard_map/last/pallas_call | solution.py:252
  (44 shorter events, 0.4 us)
Async XLA Ops:
  0.6 31.9 %collective-permute-start.3 = (f32[7,64,128]{2,1,0:T(8,128)}, f32[7,64,128]{2,1,0:T(8,128)S(1)}, u32[]{:S(2)}, u32[]{:S(2)}) collective-permute-start(f32[7,64,128]{2,1,0:T(8,128)} %bitcast.13), channel_id=1, source_target_pairs={{0,224},{32,0},{64,32},{96,64},{128,96},{160,128},{192,160},{224,1... | collective-permute-start | bytes 688136 | tf_op jit(solution)/shard_map/ppermute | solution.py:273
  7.1 25.5 %collective-permute-start = (f32[7,64,128]{2,1,0:T(8,128)}, f32[7,64,128]{2,1,0:T(8,128)S(1)}, u32[]{:S(2)}, u32[]{:S(2)}) collective-permute-start(f32[7,64,128]{2,1,0:T(8,128)} %bitcast.14), channel_id=1, source_target_pairs={{0,32},{32,64},{64,96},{96,128},{128,160},{160,192},{192,224},{224... | collective-permute-start | bytes 688136 | tf_op jit(solution)/shard_map/ppermute | solution.py:270
  7.1 1.0 copy-start
  8.3 24.2 %collective-permute-start.2 = (f32[64,128]{1,0:T(8,128)S(1)}, f32[64,128]{1,0:T(8,128)S(1)}, u32[]{:S(2)}, u32[]{:S(2)}) collective-permute-start(f32[64,128]{1,0:T(8,128)S(1)} %get-tuple-element.41), channel_id=1, source_target_pairs={{0,1},{1,2},{2,3},{3,0},{4,5},{5,6},{6,7},{7,4},{8,9},{9,10},{10,1... | collective-permute-start | bytes 98312 | tf_op jit(solution)/shard_map/ppermute | solution.py:272
  9.7 22.8 %collective-permute-start.5 = (f32[64,128]{1,0:T(8,128)S(1)}, f32[64,128]{1,0:T(8,128)S(1)}, u32[]{:S(2)}, u32[]{:S(2)}) collective-permute-start(f32[64,128]{1,0:T(8,128)S(1)} %get-tuple-element.43), channel_id=1, source_target_pairs={{0,3},{1,0},{2,1},{3,2},{4,7},{5,4},{6,5},{7,6},{8,11},{9,8},{10,9... | collective-permute-start | bytes 98312 | tf_op jit(solution)/shard_map/ppermute | solution.py:275
  11.2 3.2 %collective-permute-start.1 = (f32[8,128]{1,0:T(8,128)S(1)}, f32[8,128]{1,0:T(8,128)S(1)}, u32[]{:S(2)}, u32[]{:S(2)}) collective-permute-start(f32[8,128]{1,0:T(8,128)S(1)} %get-tuple-element.40), channel_id=1, source_target_pairs={{0,4},{4,8},{8,12},{12,16},{16,20},{20,24},{24,28},{28,0},{1,5},{5... | collective-permute-start | bytes 12296 | tf_op jit(solution)/shard_map/ppermute | solution.py:271
  14.4 18.1 %collective-permute-start.4 = (f32[8,128]{1,0:T(8,128)S(1)}, f32[8,128]{1,0:T(8,128)S(1)}, u32[]{:S(2)}, u32[]{:S(2)}) collective-permute-start(f32[8,128]{1,0:T(8,128)S(1)} %get-tuple-element.42), channel_id=1, source_target_pairs={{0,28},{4,0},{8,4},{12,8},{16,12},{20,16},{24,20},{28,24},{1,29},{... | collective-permute-start | bytes 12296 | tf_op jit(solution)/shard_map/ppermute | solution.py:274
  16.8 0.9 copy-start.1
  17.8 1.4 %copy-start.3 = (f32[1,46,64,128]{3,2,1,0:T(8,128)S(1)}, f32[1,46,64,128]{3,2,1,0:T(8,128)}, u32[]{:S(2)}) copy-start(f32[1,46,64,128]{3,2,1,0:T(8,128)} %observed.1) | copy-start | bytes 4521988
  19.2 1.4 %copy-start.4 = (s32[1,46,64,128]{3,2,1,0:T(8,128)S(1)}, s32[1,46,64,128]{3,2,1,0:T(8,128)}, u32[]{:S(2)}) copy-start(s32[1,46,64,128]{3,2,1,0:T(8,128)} %quality.1) | copy-start | bytes 4521988
  20.5 0.8 copy-start.5
  21.3 0.7 copy-start.6
  22.0 0.7 copy-start.8
  34.5 11.6 %collective-permute-start.9 = (f32[7,64,128]{2,1,0:T(8,128)S(1)}, f32[7,64,128]{2,1,0:T(8,128)S(1)}, u32[]{:S(2)}, u32[]{:S(2)}) collective-permute-start(f32[7,64,128]{2,1,0:T(8,128)S(1)} %get-tuple-element.44.last.refs_4_), channel_id=1, source_target_pairs={{0,224},{32,0},{64,32},{96,64},{128,96},{160,128},{192,160},{224,1... | collective-permute-start | bytes 688136 | tf_op jit(solution)/shard_map/ppermute | solution.py:273
  37.5 8.6 %collective-permute-start.6 = (f32[7,64,128]{2,1,0:T(8,128)S(1)}, f32[7,64,128]{2,1,0:T(8,128)S(1)}, u32[]{:S(2)}, u32[]{:S(2)}) collective-permute-start(f32[7,64,128]{2,1,0:T(8,128)S(1)} %get-tuple-element.44.last.refs_4_), channel_id=1, source_target_pairs={{0,32},{32,64},{64,96},{96,128},{128,160},{160,192},{192,224},{224... | collective-permute-start | bytes 688136 | tf_op jit(solution)/shard_map/ppermute | solution.py:270
  37.5 8.6 %collective-permute-start.8 = (f32[64,128]{1,0:T(8,128)S(1)}, f32[64,128]{1,0:T(8,128)S(1)}, u32[]{:S(2)}, u32[]{:S(2)}) collective-permute-start(f32[64,128]{1,0:T(8,128)S(1)} %get-tuple-element.46), channel_id=1, source_target_pairs={{0,1},{1,2},{2,3},{3,0},{4,5},{5,6},{6,7},{7,4},{8,9},{9,10},{10,1... | collective-permute-start | bytes 98312 | tf_op jit(solution)/shard_map/ppermute | solution.py:272
  37.6 8.5 %collective-permute-start.11 = (f32[64,128]{1,0:T(8,128)S(1)}, f32[64,128]{1,0:T(8,128)S(1)}, u32[]{:S(2)}, u32[]{:S(2)}) collective-permute-start(f32[64,128]{1,0:T(8,128)S(1)} %get-tuple-element.48), channel_id=1, source_target_pairs={{0,3},{1,0},{2,1},{3,2},{4,7},{5,4},{6,5},{7,6},{8,11},{9,8},{10,9... | collective-permute-start | bytes 98312 | tf_op jit(solution)/shard_map/ppermute | solution.py:275
  40.2 1.5 %collective-permute-start.7 = (f32[8,128]{1,0:T(8,128)S(1)}, f32[8,128]{1,0:T(8,128)S(1)}, u32[]{:S(2)}, u32[]{:S(2)}) collective-permute-start(f32[8,128]{1,0:T(8,128)S(1)} %get-tuple-element.45), channel_id=1, source_target_pairs={{0,4},{4,8},{8,12},{12,16},{16,20},{20,24},{24,28},{28,0},{1,5},{5... | collective-permute-start | bytes 12296 | tf_op jit(solution)/shard_map/ppermute | solution.py:271
  41.7 4.4 %collective-permute-start.10 = (f32[8,128]{1,0:T(8,128)S(1)}, f32[8,128]{1,0:T(8,128)S(1)}, u32[]{:S(2)}, u32[]{:S(2)}) collective-permute-start(f32[8,128]{1,0:T(8,128)S(1)} %get-tuple-element.47), channel_id=1, source_target_pairs={{0,28},{4,0},{8,4},{12,8},{16,12},{20,16},{24,20},{28,24},{1,29},{... | collective-permute-start | bytes 12296 | tf_op jit(solution)/shard_map/ppermute | solution.py:274
  48.1 12.1 %collective-permute-start.15 = (f32[7,64,128]{2,1,0:T(8,128)S(1)}, f32[7,64,128]{2,1,0:T(8,128)S(1)}, u32[]{:S(2)}, u32[]{:S(2)}) collective-permute-start(f32[7,64,128]{2,1,0:T(8,128)S(1)} %get-tuple-element.49.last.refs_5_), channel_id=1, source_target_pairs={{0,224},{32,0},{64,32},{96,64},{128,96},{160,128},{192,160},{224,1... | collective-permute-start | bytes 688136 | tf_op jit(solution)/shard_map/ppermute | solution.py:273
  51.1 9.1 %collective-permute-start.12 = (f32[7,64,128]{2,1,0:T(8,128)S(1)}, f32[7,64,128]{2,1,0:T(8,128)S(1)}, u32[]{:S(2)}, u32[]{:S(2)}) collective-permute-start(f32[7,64,128]{2,1,0:T(8,128)S(1)} %get-tuple-element.49.last.refs_5_), channel_id=1, source_target_pairs={{0,32},{32,64},{64,96},{96,128},{128,160},{160,192},{192,224},{224... | collective-permute-start | bytes 688136 | tf_op jit(solution)/shard_map/ppermute | solution.py:270
  51.1 9.1 %collective-permute-start.14 = (f32[64,128]{1,0:T(8,128)S(1)}, f32[64,128]{1,0:T(8,128)S(1)}, u32[]{:S(2)}, u32[]{:S(2)}) collective-permute-start(f32[64,128]{1,0:T(8,128)S(1)} %get-tuple-element.51), channel_id=1, source_target_pairs={{0,1},{1,2},{2,3},{3,0},{4,5},{5,6},{6,7},{7,4},{8,9},{9,10},{10,1... | collective-permute-start | bytes 98312 | tf_op jit(solution)/shard_map/ppermute | solution.py:272
  51.1 9.1 %collective-permute-start.17 = (f32[64,128]{1,0:T(8,128)S(1)}, f32[64,128]{1,0:T(8,128)S(1)}, u32[]{:S(2)}, u32[]{:S(2)}) collective-permute-start(f32[64,128]{1,0:T(8,128)S(1)} %get-tuple-element.53), channel_id=1, source_target_pairs={{0,3},{1,0},{2,1},{3,2},{4,7},{5,4},{6,5},{7,6},{8,11},{9,8},{10,9... | collective-permute-start | bytes 98312 | tf_op jit(solution)/shard_map/ppermute | solution.py:275
  53.8 2.0 %collective-permute-start.13 = (f32[8,128]{1,0:T(8,128)S(1)}, f32[8,128]{1,0:T(8,128)S(1)}, u32[]{:S(2)}, u32[]{:S(2)}) collective-permute-start(f32[8,128]{1,0:T(8,128)S(1)} %get-tuple-element.50), channel_id=1, source_target_pairs={{0,4},{4,8},{8,12},{12,16},{16,20},{20,24},{24,28},{28,0},{1,5},{5... | collective-permute-start | bytes 12296 | tf_op jit(solution)/shard_map/ppermute | solution.py:271
  55.8 4.4 %collective-permute-start.16 = (f32[8,128]{1,0:T(8,128)S(1)}, f32[8,128]{1,0:T(8,128)S(1)}, u32[]{:S(2)}, u32[]{:S(2)}) collective-permute-start(f32[8,128]{1,0:T(8,128)S(1)} %get-tuple-element.52), channel_id=1, source_target_pairs={{0,28},{4,0},{8,4},{12,8},{16,12},{20,16},{24,20},{28,24},{1,29},{... | collective-permute-start | bytes 12296 | tf_op jit(solution)/shard_map/ppermute | solution.py:274
  62.2 43.2 %copy-start.2 = (f32[1,7,64,128]{3,2,1,0:T(8,128)S(1)}, f32[1,7,64,128]{3,2,1,0:T(8,128)}, u32[]{:S(2)}) copy-start(f32[1,7,64,128]{3,2,1,0:T(8,128)} %params.1) | copy-start | bytes 688132
  62.2 43.2 %copy-start.7 = (f32[7]{0:T(128)S(1)}, f32[7]{0:T(128)}, u32[]{:S(2)}) copy-start(f32[7]{0:T(128)} %sw.13) | copy-start | bytes 88
  62.2 43.1 %copy-start.9 = (f32[7]{0:T(128)S(1)}, f32[7]{0:T(128)}, u32[]{:S(2)}) copy-start(f32[7]{0:T(128)} %tw.13) | copy-start | bytes 88
  62.2 12.1 %collective-permute-start.21 = (f32[7,64,128]{2,1,0:T(8,128)S(1)}, f32[7,64,128]{2,1,0:T(8,128)S(1)}, u32[]{:S(2)}, u32[]{:S(2)}) collective-permute-start(f32[7,64,128]{2,1,0:T(8,128)S(1)} %get-tuple-element.54.last.refs_6_), channel_id=1, source_target_pairs={{0,224},{32,0},{64,32},{96,64},{128,96},{160,128},{192,160},{224,1... | collective-permute-start | bytes 688136 | tf_op jit(solution)/shard_map/ppermute | solution.py:273
  65.2 9.1 %collective-permute-start.18 = (f32[7,64,128]{2,1,0:T(8,128)S(1)}, f32[7,64,128]{2,1,0:T(8,128)S(1)}, u32[]{:S(2)}, u32[]{:S(2)}) collective-permute-start(f32[7,64,128]{2,1,0:T(8,128)S(1)} %get-tuple-element.54.last.refs_6_), channel_id=1, source_target_pairs={{0,32},{32,64},{64,96},{96,128},{128,160},{160,192},{192,224},{224... | collective-permute-start | bytes 688136 | tf_op jit(solution)/shard_map/ppermute | solution.py:270
  65.3 9.1 %collective-permute-start.20 = (f32[64,128]{1,0:T(8,128)S(1)}, f32[64,128]{1,0:T(8,128)S(1)}, u32[]{:S(2)}, u32[]{:S(2)}) collective-permute-start(f32[64,128]{1,0:T(8,128)S(1)} %get-tuple-element.56), channel_id=1, source_target_pairs={{0,1},{1,2},{2,3},{3,0},{4,5},{5,6},{6,7},{7,4},{8,9},{9,10},{10,1... | collective-permute-start | bytes 98312 | tf_op jit(solution)/shard_map/ppermute | solution.py:272
  65.3 9.1 %collective-permute-start.23 = (f32[64,128]{1,0:T(8,128)S(1)}, f32[64,128]{1,0:T(8,128)S(1)}, u32[]{:S(2)}, u32[]{:S(2)}) collective-permute-start(f32[64,128]{1,0:T(8,128)S(1)} %get-tuple-element.58), channel_id=1, source_target_pairs={{0,3},{1,0},{2,1},{3,2},{4,7},{5,4},{6,5},{7,6},{8,11},{9,8},{10,9... | collective-permute-start | bytes 98312 | tf_op jit(solution)/shard_map/ppermute | solution.py:275
  67.9 2.0 %collective-permute-start.19 = (f32[8,128]{1,0:T(8,128)S(1)}, f32[8,128]{1,0:T(8,128)S(1)}, u32[]{:S(2)}, u32[]{:S(2)}) collective-permute-start(f32[8,128]{1,0:T(8,128)S(1)} %get-tuple-element.55), channel_id=1, source_target_pairs={{0,4},{4,8},{8,12},{12,16},{16,20},{20,24},{24,28},{28,0},{1,5},{5... | collective-permute-start | bytes 12296 | tf_op jit(solution)/shard_map/ppermute | solution.py:271
  69.9 4.4 %collective-permute-start.22 = (f32[8,128]{1,0:T(8,128)S(1)}, f32[8,128]{1,0:T(8,128)S(1)}, u32[]{:S(2)}, u32[]{:S(2)}) collective-permute-start(f32[8,128]{1,0:T(8,128)S(1)} %get-tuple-element.57), channel_id=1, source_target_pairs={{0,28},{4,0},{8,4},{12,8},{16,12},{20,16},{24,20},{28,24},{1,29},{... | collective-permute-start | bytes 12296 | tf_op jit(solution)/shard_map/ppermute | solution.py:274
  76.3 8.5 %collective-permute-start.24 = (f32[7,64,128]{2,1,0:T(8,128)S(1)}, f32[7,64,128]{2,1,0:T(8,128)S(1)}, u32[]{:S(2)}, u32[]{:S(2)}) collective-permute-start(f32[7,64,128]{2,1,0:T(8,128)S(1)} %get-tuple-element.59.v.refs_7_), channel_id=1, source_target_pairs={{0,32},{32,64},{64,96},{96,128},{128,160},{160,192},{192,224},{224... | collective-permute-start | bytes 688136 | tf_op jit(solution)/shard_map/ppermute | solution.py:270
  76.4 4.1 %collective-permute-start.26 = (f32[64,128]{1,0:T(8,128)S(1)}, f32[64,128]{1,0:T(8,128)S(1)}, u32[]{:S(2)}, u32[]{:S(2)}) collective-permute-start(f32[64,128]{1,0:T(8,128)S(1)} %get-tuple-element.61), channel_id=1, source_target_pairs={{0,1},{1,2},{2,3},{3,0},{4,5},{5,6},{6,7},{7,4},{8,9},{9,10},{10,1... | collective-permute-start | bytes 98312 | tf_op jit(solution)/shard_map/ppermute | solution.py:272
  76.5 1.2 %collective-permute-start.25 = (f32[8,128]{1,0:T(8,128)S(1)}, f32[8,128]{1,0:T(8,128)S(1)}, u32[]{:S(2)}, u32[]{:S(2)}) collective-permute-start(f32[8,128]{1,0:T(8,128)S(1)} %get-tuple-element.60), channel_id=1, source_target_pairs={{0,4},{4,8},{8,12},{12,16},{16,20},{20,24},{24,28},{28,0},{1,5},{5... | collective-permute-start | bytes 12296 | tf_op jit(solution)/shard_map/ppermute | solution.py:271
  86.5 18.9 %all-to-all-start = ((f32[256,1,128]{2,1,0:T(1,128)}), f32[256,1,128]{2,1,0:T(1,128)S(1)}, u32[]{:S(2)}, u32[]{:S(2)}) async-start(f32[256,1,128]{2,1,0:T(1,128)} %bitcast.8), calls=%async_computation | async-start | bytes 262144 | tf_op jit(solution)/shard_map/all_to_all | solution.py:326
  92.5 10.7 %collective-permute-start.27 = (f32[7,64,128]{2,1,0:T(8,128)S(1)}, f32[7,64,128]{2,1,0:T(8,128)S(1)}, u32[]{:S(2)}, u32[]{:S(2)}) collective-permute-start(f32[7,64,128]{2,1,0:T(8,128)S(1)} %get-tuple-element.59.v.refs_7_), channel_id=1, source_target_pairs={{0,224},{32,0},{64,32},{96,64},{128,96},{160,128},{192,160},{224,1... | collective-permute-start | bytes 688136 | tf_op jit(solution)/shard_map/ppermute | solution.py:273
  97.1 6.2 %collective-permute-start.29 = (f32[64,128]{1,0:T(8,128)S(1)}, f32[64,128]{1,0:T(8,128)S(1)}, u32[]{:S(2)}, u32[]{:S(2)}) collective-permute-start(f32[64,128]{1,0:T(8,128)S(1)} %get-tuple-element.71), channel_id=1, source_target_pairs={{0,3},{1,0},{2,1},{3,2},{4,7},{5,4},{6,5},{7,6},{8,11},{9,8},{10,9... | collective-permute-start | bytes 98312 | tf_op jit(solution)/shard_map/ppermute | solution.py:275
  99.7 3.6 %collective-permute-start.28 = (f32[8,128]{1,0:T(8,128)S(1)}, f32[8,128]{1,0:T(8,128)S(1)}, u32[]{:S(2)}, u32[]{:S(2)}) collective-permute-start(f32[8,128]{1,0:T(8,128)S(1)} %get-tuple-element.70), channel_id=1, source_target_pairs={{0,28},{4,0},{8,4},{12,8},{16,12},{20,16},{24,20},{28,24},{1,29},{... | collective-permute-start | bytes 12296 | tf_op jit(solution)/shard_map/ppermute | solution.py:274
